TPU v7x, 256 devices: a whole 4x4x8 slice. The times are simulated.
256 devices in a mesh: ctx: 32 (over z, x_hi, core), kvh: 8 (over y, x_lo).
Axes of the slice: x: 4 (x_hi: 2, x_lo: 2; x = x_hi * 2 + x_lo), y: 4, z: 8, core: 2. Of those that a mesh axis runs over, the one named last changes fastest.
Arguments:
- queries: bfloat16 [512, 128, 128], P('ctx', 'kvh'), may hold values from -60 to 60
- cache_keys: bfloat16 [32768, 8, 128], P('ctx', 'kvh'), may hold values from -30 to 30
- cache_values: bfloat16 [32768, 8, 128], P('ctx', 'kvh'), may hold values from -6 to 6
- new_keys: bfloat16 [512, 8, 128], P('ctx', 'kvh'), may hold values from -8 to 8
- new_values: bfloat16 [512, 8, 128], P('ctx', 'kvh'), may hold values from -6 to 6
- fill_rows: int32 [32], P('ctx'), may hold values from 128 to 1024, as said below
- turn_start: int32 [1], replicated, may hold values from 1024 to 4095
- out_weight: bfloat16 [16384, 16384], P('kvh', 'ctx'), may hold values from -0.046875 to 0.046875
Outputs:
- mixed: bfloat16 [512, 16384], P('kvh', 'ctx')
Inputs may be any that keep to these rules, and one draw needn't show every extreme that they name: `fill_rows`: each is a multiple of 128; some shard is full.
All inputs are finite; a program needn't handle non-finite values.
Results may differ from a plain program's by a relative error of at most 0.02.
Values may be sent and summed in bfloat16 or wider, within the bound.
No kernel may reach another device: no remote copies, remote signals or barrier semaphores. Data moves between devices by JAX's collectives and lax.ppermute only.
A program may use at most 64 MiB of HBM per device.

v0:
```python
import math

import jax
import jax.numpy as jnp
from jax import lax
from jax.sharding import PartitionSpec as P

NEG = -1e30
ROPE_BASE = 500000.0


def rotate(values, positions):
    half_width = values.shape[-1] // 2
    steps_index = jnp.arange(half_width, dtype=jnp.float32)
    inverse = jnp.exp(steps_index * (-2.0 * math.log(ROPE_BASE) / values.shape[-1]))
    angles = positions[:, None] * inverse[None, :]
    cosine = jnp.cos(angles)[:, None, :]
    sine = jnp.sin(angles)[:, None, :]
    first_half = values[..., :half_width].astype(jnp.float32)
    second_half = values[..., half_width:].astype(jnp.float32)
    return jnp.concatenate(
        [first_half * cosine - second_half * sine, second_half * cosine + first_half * sine],
        axis=-1,
    ).astype(jnp.bfloat16)


def attend(running, flat_queries, key_slab, value_slab, allowed):
    old_max, old_total, old_output = running
    score_scale = flat_queries.shape[1] ** (-0.5)
    scores = (
        jnp.einsum("rd,kd->rk", flat_queries, key_slab, preferred_element_type=jnp.float32)
        * score_scale
    )
    scores = jnp.where(allowed, scores, NEG)
    new_max = jnp.maximum(old_max, scores.max(axis=-1))
    rescale = jnp.exp(old_max - new_max)
    weights_bf = jnp.where(allowed, jnp.exp(scores - new_max[:, None]), 0.0).astype(jnp.bfloat16)
    new_total = rescale * old_total + weights_bf.astype(jnp.float32).sum(axis=-1)
    new_output = rescale[:, None] * old_output + jnp.dot(
        weights_bf, value_slab, preferred_element_type=jnp.float32
    )
    return (new_max, new_total, new_output)


def blank_state(total_rows, head_width):
    return (
        jnp.full((total_rows,), NEG, jnp.float32),
        jnp.zeros((total_rows,), jnp.float32),
        jnp.zeros((total_rows, head_width), jnp.float32),
    )


def cache_pass(flat_queries, cached_keys, cached_values, fill_count, block_count, key_block):
    initial = blank_state(flat_queries.shape[0], flat_queries.shape[1])

    def one_block(block_index, running):
        begin = block_index * key_block
        key_slab = lax.dynamic_slice_in_dim(cached_keys, begin, key_block, 0)
        value_slab = lax.dynamic_slice_in_dim(cached_values, begin, key_block, 0)
        allowed = (begin + jnp.arange(key_block, dtype=jnp.int32) < fill_count)[None, :]
        return attend(running, flat_queries, key_slab, value_slab, allowed)

    return lax.fori_loop(0, block_count, one_block, initial)


def on_device(
    queries, cache_keys, cache_values, new_keys, new_values, fill_rows, turn_start, out_weight
):
    tok_dev, group_size, head_width = queries.shape
    ctx_count = lax.axis_size("ctx")
    my_index = lax.axis_index("ctx")
    cache_rows = cache_keys.shape[0]
    turn_rows = tok_dev * ctx_count
    key_block = min(256, cache_rows)
    cached_keys = cache_keys.reshape(cache_rows, head_width)
    cached_values = cache_values.reshape(cache_rows, head_width)
    local_tokens = my_index * tok_dev + jnp.arange(tok_dev, dtype=jnp.int32)
    positions = (turn_start[0] + local_tokens).astype(jnp.float32)
    turned_queries = rotate(queries, positions).reshape(tok_dev, group_size * head_width)
    turned_keys = rotate(new_keys, positions).reshape(tok_dev, head_width)
    fresh_values = new_values.reshape(tok_dev, head_width)
    fill_count = fill_rows[0]
    block_count = (fill_count + key_block - 1) // key_block
    own_tokens = (
        my_index * tok_dev + jnp.arange(tok_dev * group_size, dtype=jnp.int32) // group_size
    )
    all_keys, all_values = (
        lax.all_gather(turned_keys, "ctx", axis=0, tiled=True),
        lax.all_gather(fresh_values, "ctx", axis=0, tiled=True),
    )
    own_queries = turned_queries.reshape(tok_dev * group_size, head_width)
    own_allowed = jnp.arange(turn_rows, dtype=jnp.int32)[None, :] <= own_tokens[:, None]
    own_state = attend(
        blank_state(tok_dev * group_size, head_width),
        own_queries,
        all_keys,
        all_values,
        own_allowed,
    )
    shard_piece = lax.all_gather(turned_queries, "ctx", axis=0, tiled=True)
    piece_rows = shard_piece.shape[0]
    flat_queries = shard_piece.reshape(piece_rows * group_size, head_width)
    running = cache_pass(
        flat_queries, cached_keys, cached_values, fill_count, block_count, key_block
    )
    max_rows = running[0].reshape(piece_rows, group_size)
    total_rows = running[1].reshape(piece_rows, group_size)
    output_rows = running[2].reshape(piece_rows, group_size, head_width)
    got_max, got_total, got_output = (
        lax.all_to_all(max_rows, "ctx", split_axis=0, concat_axis=0, tiled=True),
        lax.all_to_all(total_rows, "ctx", split_axis=0, concat_axis=0, tiled=True),
        lax.all_to_all(output_rows, "ctx", split_axis=0, concat_axis=0, tiled=True),
    )
    got_max = got_max.reshape(ctx_count, tok_dev, group_size)
    got_total = got_total.reshape(ctx_count, tok_dev, group_size)
    got_output = got_output.reshape(ctx_count, tok_dev, group_size, head_width)
    row_top = got_max.max(axis=0)
    rescale = jnp.exp(got_max - row_top[None])
    sum_total = (rescale * got_total).sum(axis=0)
    sum_output = (rescale[..., None] * got_output).sum(axis=0)
    own_max = own_state[0].reshape(tok_dev, group_size)
    own_total = own_state[1].reshape(tok_dev, group_size)
    own_output = own_state[2].reshape(tok_dev, group_size, head_width)
    new_top = jnp.maximum(row_top, own_max)
    shift_old = jnp.exp(row_top - new_top)
    shift_own = jnp.exp(own_max - new_top)
    sum_total = shift_old * sum_total + shift_own * own_total
    sum_output = shift_old[..., None] * sum_output + shift_own[..., None] * own_output
    attention = (
        (sum_output / sum_total[..., None])
        .astype(jnp.bfloat16)
        .reshape(tok_dev, group_size * head_width)
    )
    head_terms = jnp.dot(
        lax.all_gather(attention, "ctx", axis=0, tiled=True),
        out_weight,
        preferred_element_type=jnp.float32,
    )
    return lax.psum_scatter(head_terms.astype(jnp.bfloat16), "kvh", scatter_dimension=0, tiled=True)


def solution(mesh):
    in_specs = (
        P("ctx", "kvh", None),
        P("ctx", "kvh", None),
        P("ctx", "kvh", None),
        P("ctx", "kvh", None),
        P("ctx", "kvh", None),
        P("ctx"),
        P(),
        P("kvh", "ctx"),
    )
    out_specs = P("kvh", "ctx")
    return jax.shard_map(
        on_device, mesh=mesh, in_specs=in_specs, out_specs=out_specs, check_vma=False
    )
```

profile of v0, /device:TPU:1, one launch (start us, length us, event | category | flops | bytes accessed | tf_op | source)
XLA Modules:
  0.0 475.5 jit_solution(11697429385140661447)
XLA Ops:
  7.4 0.1 multiply_cosine_fusion.1
  7.5 1.0 fusion.7
  8.5 0.1 pad_maximum_fusion
  8.6 0.6 copy.17
  10.0 84.4 %all-gather.4.cloned.1.call-done = bf16[512,2048]{1,0:T(8,128)(2,1)} async-done(((bf16[16,2048]{1,0:T(8,128)(2,1)}), bf16[512,2048]{1,0:T(8,128)(2,1)}) %all-gather.4.cloned.1.call-update) | async-done | bytes 2097168 | tf_op jit(solution)/shard_map/all_gather | solution.py:100
  94.3 4.2 reshape.243
  98.5 2.2 broadcast_in_dim.69
  100.7 48.0 %while.14 = (s32[]{:T(128)}, f32[8192]{0:T(1024)S(1)}, f32[8192]{0:T(1024)S(1)}, f32[8192,128]{1,0:T(8,128)}, s32[]{:T(128)}, /*index=5*/s32[]{:T(128)}, bf16[10...) while((s32[]{:T(128)}, f32[8192]{0:T(1024)S(1)}, ...), condition=%wide.region_3.4_spmd, body=%wide.region_0.3_spmd.sunk | while | flops 1098924544 | bytes 69862640 | solution.py:63
  100.7 0.7 add_compare_fusion.2
  101.4 2.9 fusion.44
  104.4 1.6 convert_reduce_fusion.3
  106.0 0.6 copy-done.1
  106.5 4.2 convolution_add_fusion.3
  110.8 1.9 copy-done.2
  112.7 0.7 add_compare_fusion.2
  113.4 2.9 fusion.44
  116.3 1.6 convert_reduce_fusion.3
  117.9 0.6 copy-done.1
  118.5 4.2 convolution_add_fusion.3
  122.8 1.9 copy-done.2
  124.7 0.7 add_compare_fusion.2
  125.4 2.9 fusion.44
  128.3 1.6 convert_reduce_fusion.3
  129.9 0.6 copy-done.1
  130.5 4.2 convolution_add_fusion.3
  134.8 1.9 copy-done.2
  136.7 0.7 add_compare_fusion.2
  137.3 2.9 fusion.44
  140.3 1.6 convert_reduce_fusion.3
  141.9 0.6 copy-done.1
  142.5 4.2 convolution_add_fusion.3
  146.8 1.9 copy-done.2
  148.7 0.1 all_to_all.15
  148.8 0.8 reshape.250
  149.6 4.5 all-to-all-start
  154.1 0.1 all_to_all.18
  154.2 0.1 reshape.252
  154.4 9.3 %all-to-all-done = f32[32,1,256]{2,1,0:T(1,128)S(1)} async-done(((f32[32,1,256]{2,1,0:T(1,128)}), f32[32,1,256]{2,1,0:T(1,128)S(1)}, u32[]{:S(2)}, u32[]{:S(2)}) %all-to-all-start) | async-done | bytes 32800 | tf_op jit(solution)/shard_map/all_to_all | solution.py:110
  163.7 12.8 %all_to_all.23 = f32[32,1,256]{2,1,0:T(1,128)S(1)} all-to-all(f32[32,1,256]{2,1,0:T(1,128)S(1)} %reshape.252), channel_id=1, replica_groups=mesh['ctx'=32,'kvh'=8] {'ctx'}, dimensions={0} | all-to-all | bytes 65536 | tf_op jit(solution)/shard_map/all_to_all | solution.py:111
  176.5 5.0 %all-to-all-start.1 = ((f32[512,16,128]{2,1,0:T(8,128)}), f32[512,16,128]{2,1,0:T(8,128)}, u32[]{:S(2)}, u32[]{:S(2)}) async-start(f32[512,16,128]{2,1,0:T(8,128)} %bitcast.43), calls=%async_computation.1 | async-start | bytes 8388608 | tf_op jit(solution)/shard_map/all_to_all | solution.py:112
  181.5 0.1 fusion.27
  181.6 0.1 pad_maximum_fusion.1
  181.7 124.4 %all_gather.13 = bf16[512,128]{1,0:T(8,128)(2,1)S(1)} all-gather(bf16[16,128]{1,0:T(8,128)(2,1)S(1)} %pad_maximum_fusion.1), channel_id=1, replica_groups=mesh['ctx'=32,'kvh'=8] {'ctx'}, dimensions={0}, use_global_device_ids=true | all-gather | bytes 135168 | tf_op jit(solution)/shard_map/all_gather | solution.py:88
  306.1 0.4 fusion.33
  306.5 0.1 max_broadcast_in_dim.27
  306.6 0.3 convert_reduce_fusion.1
  306.9 0.1 reduce_sum.41
  306.9 39.9 %all-gather = bf16[512,1,128]{2,0,1:T(8,128)(2,1)S(1)} all-gather(bf16[16,1,128]{2,0,1:T(8,128)(2,1)S(1)} %copy-done.4), channel_id=2, replica_groups=mesh['ctx'=32,'kvh'=8] {'ctx'}, dimensions={0}, use_global_device_ids=true | all-gather | bytes 135168 | tf_op jit(solution)/shard_map/all_gather | solution.py:89
  346.8 0.2 convolution_add_fusion.1
  347.1 0.5 broadcast.193
  347.6 0.7 reduce.4
  348.3 0.1 reshape.251
  348.4 0.7 reduce.3
  349.2 0.1 reshape.253
  349.3 0.1 multiply_reduce_fusion.1
  349.4 2.9 multiply_reduce_fusion
  352.3 0.1 broadcast_multiply_fusion
  352.4 0.1 mul.207
  352.5 0.1 div.32
  352.6 0.8 fusion.10
  353.4 0.0 reduce-scatter.2.cloned.1.call-start
  353.4 79.6 %all-gather.6.cloned.1.call-done = bf16[512,2048]{1,0:T(8,128)(2,1)} async-done(((bf16[16,2048]{1,0:T(8,128)(2,1)}), bf16[512,2048]{1,0:T(8,128)(2,1)}) %all-gather.6.cloned.1.call-update) | async-done | bytes 2097168 | tf_op jit(solution)/shard_map/all_gather | solution.py:135
  433.0 3.6 convolution_convert_fusion
  436.7 32.3 %reduce-scatter.2.cloned.1.call-done = bf16[64,512]{1,0:T(8,128)(2,1)} async-done(((bf16[512,512]{1,0:T(8,128)(2,1)}), bf16[64,512]{1,0:T(8,128)(2,1)}) %reduce-scatter.2.cloned.1.call-update) | async-done | bytes 65552 | tf_op jit(solution)/shard_map/reduce_scatter | solution.py:139
  (41 shorter events, 0.4 us)
Async XLA Ops:
  6.5 426.5 %copy-start = (bf16[2048,512]{1,0:T(8,128)(2,1)S(1)}, bf16[2048,512]{1,0:T(8,128)(2,1)}, u32[]{:S(2)}) copy-start(bf16[2048,512]{1,0:T(8,128)(2,1)} %param.17) | copy-start | bytes 6291460
  6.5 87.8 %all-gather.4.cloned.1.call-start = ((), (), s32[]{:S(2)}) async-start(), calls=%async_computation.4 | async-start | bytes 2162688 | tf_op jit(solution)/shard_map/all_gather | solution.py:100
  104.3 2.2 copy-start.1
  110.8 1.9 copy-start.2
  116.3 2.2 copy-start.1
  122.8 1.9 copy-start.2
  128.3 2.2 copy-start.1
  134.8 1.9 copy-start.2
  140.3 2.2 copy-start.1
  146.8 1.9 copy-start.2
  149.6 14.1 %all-to-all-start = ((f32[32,1,256]{2,1,0:T(1,128)}), f32[32,1,256]{2,1,0:T(1,128)S(1)}, u32[]{:S(2)}, u32[]{:S(2)}) async-start(f32[32,1,256]{2,1,0:T(1,128)} %reshape.250), calls=%async_computation | async-start | bytes 65536 | tf_op jit(solution)/shard_map/all_to_all | solution.py:110
  176.5 5.0 %copy-start.3 = (bf16[16,1,128]{2,0,1:T(8,128)(2,1)S(1)}, bf16[16,1,128]{2,0,1:T(8,128)(2,1)}, u32[]{:S(2)}) copy-start(bf16[16,1,128]{2,0,1:T(8,128)(2,1)} %param.13) | copy-start | bytes 12292
  176.5 130.5 %copy-start.4 = (bf16[16,1,128]{2,0,1:T(8,128)(2,1)S(1)}, bf16[16,1,128]{2,0,1:T(8,128)(2,1)}, u32[]{:S(2)}) copy-start(bf16[16,1,128]{2,0,1:T(8,128)(2,1)} %param.14) | copy-start | bytes 12292
  176.5 173.0 %all-to-all-start.1 = ((f32[512,16,128]{2,1,0:T(8,128)}), f32[512,16,128]{2,1,0:T(8,128)}, u32[]{:S(2)}, u32[]{:S(2)}) async-start(f32[512,16,128]{2,1,0:T(8,128)} %bitcast.43), calls=%async_computation.1 | async-start | bytes 8388608 | tf_op jit(solution)/shard_map/all_to_all | solution.py:112
  181.4 251.6 %all-gather.6.cloned.1.call-start = ((), (), s32[]{:S(2)}) async-start(), calls=%async_computation.5 | async-start | bytes 2162688 | tf_op jit(solution)/shard_map/all_gather | solution.py:135
  353.4 115.5 %reduce-scatter.2.cloned.1.call-start = ((), (), s32[]{:S(2)}) async-start(), calls=%async_computation.6 | async-start | bytes 589824 | tf_op jit(solution)/shard_map/reduce_scatter | solution.py:139
Sparse Core Ops, SparseCore 0:
  10.1 84.1 all-gather.3
  353.5 79.4 all-gather.5
  436.8 32.0 reduce-scatter.1
where the time goes:
time: 480 us; the launch traced here: 475 us
  waiting for transfers between devices  206 us (43%)
  blocking collectives  177 us (37%)
  matrix products  32.9 us (7%)
  local copies, waits for them, and re-layouts  19.4 us (4%)
  other arithmetic  16 us (3%)
  between operations  14.7 us (3%)
  starting transfers between devices  9.54 us (2%)
    all_gather x1, blocking collectives, on_device(): lax.all_gather(turned_keys, 'ctx', axis=0, tiled=True)  124 us
    all_gather x1, waiting for transfers between devices, on_device(): shard_piece = lax.all_gather(turned_queries, 'ctx', axis=0, tiled=True)  84.4 us
    all_gather x1, waiting for transfers between devices, on_device(): lax.all_gather(attention, 'ctx', axis=0, tiled=True)  79.6 us
    all_gather x1, blocking collectives, on_device(): lax.all_gather(fresh_values, 'ctx', axis=0, tiled=True)  39.9 us
    reduce_scatter x1, waiting for transfers between devices, on_device(): lax.psum_scatter(head_terms.astype(jnp.bfloat16), 'kvh', scatter_dimensio...  32.3 us
    dot_general x5, matrix products, attend(): jnp.dot(weights_bf, value_slab, preferred_element_type=jnp.float32)  17.2 us
    all_to_all x1, blocking collectives, on_device(): lax.all_to_all(total_rows, 'ctx', split_axis=0, concat_axis=0, tiled=True)  12.8 us
    dot_general x5, matrix products, attend(): jnp.einsum('rd,kd->rk', flat_queries, key_slab, preferred_element_type=jn...  12.1 us
  transfers between devices with their start and end apart: 5, of which 4 were waited for; matrix products, arithmetic and copies ran while one was open for 1% of the time, Pallas kernels for 0%

commit v1 on v0

v1 whole, which is shorter than its diff:
```python
import functools
import math

import jax
import jax.numpy as jnp
from jax import lax
from jax.experimental import pallas as pl
from jax.experimental.pallas import tpu as pltpu
from jax.sharding import PartitionSpec as P

NEG = -1e30
ROPE_BASE = 500000.0
LOG2E = 1.4426950408889634
HD = 128
STAT = 16
VMEM = pl.BlockSpec(memory_space=pltpu.VMEM)
SMEM = pl.BlockSpec(memory_space=pltpu.SMEM)


def rotate(values, positions):
    half_width = values.shape[-1] // 2
    steps_index = jnp.arange(half_width, dtype=jnp.float32)
    inverse = jnp.exp(steps_index * (-2.0 * math.log(ROPE_BASE) / values.shape[-1]))
    angles = positions[:, None] * inverse[None, :]
    cosine = jnp.cos(angles)[:, None, :]
    sine = jnp.sin(angles)[:, None, :]
    first_half = values[..., :half_width].astype(jnp.float32)
    second_half = values[..., half_width:].astype(jnp.float32)
    return jnp.concatenate(
        [first_half * cosine - second_half * sine, second_half * cosine + first_half * sine],
        axis=-1,
    ).astype(jnp.bfloat16)


def dot_nt(a, b):
    return lax.dot_general(a, b, (((1,), (1,)), ((), ())), preferred_element_type=jnp.float32)


def augment(v_scratch, slot, values):
    v_scratch[slot, :, :HD] = values
    v_scratch[slot, :, HD:] = jnp.ones_like(values)


def fill_bias(pack, cache_rows):
    fill = pack[2 * cache_rows + 32 : 2 * cache_rows + 48, :].astype(jnp.float32)[0:1, :]
    fill = jnp.concatenate([fill] * (cache_rows // HD), axis=1)
    row = lax.broadcasted_iota(jnp.int32, (1, cache_rows), 1).astype(jnp.float32)
    return jnp.where(row < fill, 0.0, NEG)


def first_kernel(chunks, cache_rows, *refs):
    q_refs, (pack_a, pack_b, acc_ref, top_ref, q_all, v_aug) = refs[:chunks], refs[chunks:]
    n = cache_rows
    packs = (pack_a, pack_b)
    for i in range(chunks):
        q_all[i] = q_refs[i][...]
    for s, pack in enumerate(packs):
        augment(v_aug, s, pack[n : 2 * n, :])
    scale = LOG2E / math.sqrt(HD)

    def one_chunk(i, carry):
        q = q_all[i]
        scores = [dot_nt(q, p[0:n, :]) * scale + fill_bias(p, n) for p in packs]
        top = functools.reduce(jnp.maximum, [s.max(axis=1, keepdims=True) for s in scores])
        acc = None
        for s in range(2):
            weights = jnp.exp2(scores[s] - top).astype(jnp.bfloat16)
            part = jnp.dot(weights, v_aug[s], preferred_element_type=jnp.float32)
            acc = part if acc is None else acc + part
        acc_ref[i] = acc
        top_ref[i] = jnp.broadcast_to(top, top_ref.shape[1:])
        return carry

    lax.fori_loop(0, chunks, one_chunk, 0)


def flash_first(q_list, packs, cache_rows):
    chunks = len(q_list)
    rows = q_list[0].shape[0]
    keys = 2 * cache_rows
    return pl.pallas_call(
        functools.partial(first_kernel, chunks, cache_rows),
        out_shape=(
            jax.ShapeDtypeStruct((chunks, rows, 2 * HD), jnp.float32),
            jax.ShapeDtypeStruct((chunks, rows, HD), jnp.float32),
        ),
        in_specs=[VMEM] * (chunks + 2),
        out_specs=(VMEM, VMEM),
        scratch_shapes=[
            pltpu.VMEM((chunks, rows, HD), jnp.bfloat16),
            pltpu.VMEM((2, cache_rows, 2 * HD), jnp.bfloat16),
        ],
        compiler_params=pltpu.CompilerParams(vmem_limit_bytes=36 << 20),
        cost_estimate=pl.CostEstimate(
            flops=chunks * rows * keys * HD * 8,
            bytes_accessed=4 << 20,
            transcendentals=chunks * rows * keys,
        ),
        name="flash_first",
    )(*q_list, *packs)


def second_kernel(half, cache_rows, where_ref, *refs):
    q_refs, refs = refs[: 2 * half], refs[2 * half :]
    acc_a, top_a, acc_b, top_b, pack_o, pack_c, pack_x, pack_xc, out_ref, q_all, v_aug, new_k, new_v = refs
    n = cache_rows
    for i in range(2 * half):
        q_all[i] = q_refs[i][...]
    packs = (pack_x, pack_xc)
    for s, pack in enumerate(packs):
        augment(v_aug, s, pack[n : 2 * n, :])
    new_k[...] = jnp.zeros_like(new_k)
    new_v[...] = jnp.zeros_like(new_v)
    for s, pack in enumerate((pack_o, pack_c, pack_x, pack_xc)):
        new_k[16 * s : 16 * s + 16, :] = pack[2 * n : 2 * n + 16, :]
        new_v[16 * s : 16 * s + 16, :HD] = pack[2 * n + 16 : 2 * n + 32, :]
    new_v[:, HD:] = jnp.ones((HD, HD), jnp.bfloat16)
    scale = LOG2E / math.sqrt(HD)
    rows = q_all.shape[1]
    my_z, my_x, my_c = where_ref[0], where_ref[1], where_ref[2]
    column = lax.broadcasted_iota(jnp.int32, (rows, HD), 1)
    row_token = lax.rem(lax.broadcasted_iota(jnp.int32, (rows, HD), 0), 16)
    key_token = (
        64 * my_z
        + 32 * (my_x ^ (column >> 5))
        + 16 * (my_c ^ ((column >> 4) & 1))
        + (column & 15)
    )
    key_token = jnp.where(column < 64, key_token, 1 << 20)

    def one_chunk(i, acc0, top0):
        q = q_all[i]
        dest = where_ref[3 + i]
        first_token = 64 * dest + 32 * my_x + 16 * my_c
        fresh = dot_nt(q, new_k[...]) * scale
        fresh = jnp.where(key_token <= row_token + first_token, fresh, NEG)
        scores = [dot_nt(q, p[0:n, :]) * scale + fill_bias(p, n) for p in packs]
        top = functools.reduce(
            jnp.maximum, [s.max(axis=1, keepdims=True) for s in scores + [fresh]]
        )
        top = jnp.maximum(top0, jnp.broadcast_to(top, top0.shape))
        one_top = top[:, 0:1]
        keep = jnp.exp2(top0 - top)
        acc = jnp.concatenate([keep, keep], axis=1) * acc0
        for s in range(2):
            weights = jnp.exp2(scores[s] - one_top).astype(jnp.bfloat16)
            acc = acc + jnp.dot(weights, v_aug[s], preferred_element_type=jnp.float32)
        weights = jnp.exp2(fresh - one_top).astype(jnp.bfloat16)
        acc = acc + jnp.dot(weights, new_v[...], preferred_element_type=jnp.float32)
        total = acc[:, HD:]
        out_ref[dest, 0:rows, :] = (acc[:, :HD] / total).astype(jnp.bfloat16)
        level = top + jnp.log2(total)
        stat = jnp.zeros((STAT, HD), jnp.float32)
        line = lax.broadcasted_iota(jnp.int32, (STAT, HD), 0)
        for b in range(rows // HD):
            flat = jnp.transpose(level[b * HD : (b + 1) * HD, :])[0:STAT, :]
            for t in range(3):
                piece = flat.astype(jnp.bfloat16).astype(jnp.float32)
                stat = jnp.where(line == 3 * b + t, piece, stat)
                flat = flat - piece
        out_ref[dest, rows : rows + STAT, :] = stat.astype(jnp.bfloat16)

    def loop_a(i, carry):
        one_chunk(i, acc_a[i], top_a[i])
        return carry

    def loop_b(i, carry):
        one_chunk(i + half, acc_b[i], top_b[i])
        return carry

    lax.fori_loop(0, half, loop_a, 0)
    lax.fori_loop(0, half, loop_b, 0)


def flash_second(where, q_list, state_a, state_b, packs, cache_rows):
    chunks = len(q_list)
    rows = q_list[0].shape[0]
    keys = 2 * cache_rows + HD
    return pl.pallas_call(
        functools.partial(second_kernel, chunks // 2, cache_rows),
        out_shape=jax.ShapeDtypeStruct((chunks, rows + STAT, HD), jnp.bfloat16),
        in_specs=[SMEM] + [VMEM] * (chunks + 8),
        out_specs=VMEM,
        scratch_shapes=[
            pltpu.VMEM((chunks, rows, HD), jnp.bfloat16),
            pltpu.VMEM((2, cache_rows, 2 * HD), jnp.bfloat16),
            pltpu.VMEM((HD, HD), jnp.bfloat16),
            pltpu.VMEM((HD, 2 * HD), jnp.bfloat16),
        ],
        compiler_params=pltpu.CompilerParams(vmem_limit_bytes=36 << 20),
        cost_estimate=pl.CostEstimate(
            flops=chunks * rows * keys * HD * 8,
            bytes_accessed=8 << 20,
            transcendentals=chunks * rows * keys,
        ),
        name="flash_second",
    )(where, *q_list, *state_a, *state_b, *packs)


def merge_kernel(in_ref, out_ref):
    shards = in_ref.shape[0]
    rows = out_ref.shape[0]
    for b in range(rows // HD):
        levels = []
        for s in range(shards):
            stat = in_ref[s, rows : rows + STAT, :].astype(jnp.float32)
            flat = stat[3 * b : 3 * b + 1] + stat[3 * b + 1 : 3 * b + 2] + stat[3 * b + 2 : 3 * b + 3]
            levels.append(jnp.transpose(jnp.broadcast_to(flat, (HD, HD))))
        top = functools.reduce(jnp.maximum, levels)
        total = jnp.zeros((HD, HD), jnp.float32)
        acc = jnp.zeros((HD, HD), jnp.float32)
        for s in range(shards):
            share = jnp.exp2(levels[s] - top)
            total = total + share
            acc = acc + share * in_ref[s, b * HD : (b + 1) * HD, :].astype(jnp.float32)
        out_ref[b * HD : (b + 1) * HD, :] = (acc / total).astype(jnp.bfloat16)


def merge(got):
    rows = got.shape[1] - STAT
    return pl.pallas_call(
        merge_kernel,
        out_shape=jax.ShapeDtypeStruct((rows, HD), jnp.bfloat16),
        in_specs=[VMEM],
        out_specs=VMEM,
        compiler_params=pltpu.CompilerParams(vmem_limit_bytes=16 << 20),
        cost_estimate=pl.CostEstimate(
            flops=4 << 20, bytes_accessed=1 << 20, transcendentals=1 << 18
        ),
        name="merge",
    )(got)


def project_kernel(chunks, where_ref, *refs):
    pair_refs, (w_own, w_core, out_ref, rows_scratch) = refs[:chunks], refs[chunks:]
    my_x = where_ref[1]
    heads = rows_scratch.shape[3] // HD
    for i in range(chunks):
        dest = where_ref[3 + i]
        for k in range(2):
            side = my_x ^ k
            for h in range(heads):
                rows_scratch[dest, side, :, h * HD : (h + 1) * HD] = pair_refs[i][
                    (k * heads + h) * 16 : (k * heads + h) * 16 + 16, :
                ]
    left = rows_scratch[...].reshape(chunks * 32, heads * HD)
    width = w_own.shape[1]
    for k, w in enumerate((w_own, w_core)):
        terms = jnp.dot(left, w[...], preferred_element_type=jnp.float32)
        out_ref[:, :, k * width : (k + 1) * width] = terms.astype(jnp.bfloat16).reshape(
            chunks, 32, width
        )


def project(where, pairs, w_own, w_core):
    chunks = len(pairs)
    depth, width = w_own.shape
    return pl.pallas_call(
        functools.partial(project_kernel, chunks),
        out_shape=jax.ShapeDtypeStruct((chunks, 32, 2 * width), jnp.bfloat16),
        in_specs=[SMEM] + [VMEM] * (chunks + 2),
        out_specs=VMEM,
        scratch_shapes=[pltpu.VMEM((chunks, 2, 16, depth), jnp.bfloat16)],
        compiler_params=pltpu.CompilerParams(vmem_limit_bytes=24 << 20),
        cost_estimate=pl.CostEstimate(
            flops=2 * chunks * 32 * depth * 2 * width, bytes_accessed=6 << 20, transcendentals=0
        ),
        name="project",
    )(where, *pairs, w_own, w_core)


ORDER = (0, 1, 7, 2, 6, 3, 5, 4)


def on_device(
    queries, cache_keys, cache_values, new_keys, new_values, fill_rows, turn_start, out_weight
):
    tok_dev, group_size, head_width = queries.shape
    ctx_count = lax.axis_size("ctx")
    z_count = ctx_count // 4
    kvh_count = lax.axis_size("kvh")
    me = lax.axis_index("ctx")
    my_z, my_x, my_c = me // 4, (me // 2) % 2, me % 2
    cache_rows = cache_keys.shape[0]

    def permutation(target):
        return [
            ((z * 2 + x) * 2 + c, (target(z, x, c)[0] * 2 + target(z, x, c)[1]) * 2 + target(z, x, c)[2])
            for z in range(z_count)
            for x in range(2)
            for c in range(2)
        ]

    to_core = permutation(lambda z, x, c: (z, x, 1 - c))
    to_x = permutation(lambda z, x, c: (z, 1 - x, c))
    to_up = permutation(lambda z, x, c: ((z + 1) % z_count, x, c))
    to_down = permutation(lambda z, x, c: ((z - 1) % z_count, x, c))

    def send(value, where_to):
        return lax.ppermute(value, "ctx", where_to)

    def ring(own):
        by_offset = {0: own}
        from_below, from_above = own, own
        for step in range(1, z_count // 2 + 1):
            from_below = send(from_below, to_up)
            by_offset[z_count - step] = from_below
            if step < z_count // 2:
                from_above = send(from_above, to_down)
                by_offset[step] = from_above
        return [by_offset[d] for d in ORDER]

    positions = (turn_start[0] + me * tok_dev + jnp.arange(tok_dev, dtype=jnp.int32)).astype(
        jnp.float32
    )
    own_queries = (
        rotate(queries, positions).transpose(1, 0, 2).reshape(group_size * tok_dev, head_width)
    )
    turned_keys = rotate(new_keys, positions).reshape(tok_dev, head_width)
    fill_block = jnp.full((16, head_width), fill_rows[0].astype(jnp.bfloat16))
    pack = jnp.concatenate(
        [
            cache_keys.reshape(cache_rows, head_width),
            cache_values.reshape(cache_rows, head_width),
            turned_keys,
            new_values.reshape(tok_dev, head_width),
            fill_block,
        ],
        axis=0,
    )
    pack_x = send(pack, to_x)
    pack_c = send(pack, to_core)
    pack_xc = send(pack_x, to_core)
    w_core = send(out_weight, to_core)
    where = jnp.concatenate(
        [
            jnp.stack([my_z, my_x, my_c]),
            (my_z + jnp.asarray(ORDER, jnp.int32)) % z_count,
        ]
    ).astype(jnp.int32)

    gathered = ring(own_queries)
    half = z_count // 2
    state_a = flash_first(gathered[:half], (pack, pack_c), cache_rows)
    state_b = flash_first(gathered[half:], (pack, pack_c), cache_rows)
    partial = flash_second(
        where, gathered, state_a, state_b, (pack, pack_c, pack_x, pack_xc), cache_rows
    )
    z_groups = [
        [(z * 2 + x) * 2 + c for z in range(z_count)] for x in range(2) for c in range(2)
    ]
    got = lax.all_to_all(partial, "ctx", 0, 0, axis_index_groups=z_groups, tiled=True)
    attention = merge(got)
    pair = jnp.concatenate([attention, send(attention, to_x)], axis=0)
    pairs = ring(pair)
    terms = project(where, pairs, out_weight, w_core)
    summed = (
        lax.all_to_all(terms, "kvh", 0, 0, tiled=True)
        .astype(jnp.float32)
        .sum(axis=0)
        .astype(jnp.bfloat16)
    )
    width = out_weight.shape[1]
    mine = summed[:, :width].reshape(2, 1, tok_dev, width)
    other = send(summed[:, width:], to_core).reshape(2, 1, tok_dev, width)
    ordered = jnp.where(
        my_c == 0,
        jnp.concatenate([mine, other], axis=1),
        jnp.concatenate([other, mine], axis=1),
    )
    return ordered.reshape(4 * tok_dev, width)


def solution(mesh):
    in_specs = (
        P("ctx", "kvh", None),
        P("ctx", "kvh", None),
        P("ctx", "kvh", None),
        P("ctx", "kvh", None),
        P("ctx", "kvh", None),
        P("ctx"),
        P(),
        P("kvh", "ctx"),
    )
    out_specs = P("kvh", "ctx")
    return jax.shard_map(
        on_device, mesh=mesh, in_specs=in_specs, out_specs=out_specs, check_vma=False
    )
```

time: 480 us -> 136 us (0.28)
  waiting for transfers between devices: 206 us -> 21.2 us
  blocking collectives: 177 us -> 31.8 us
  starting transfers between devices: 9.54 us -> 43.3 us
  matrix products: 32.9 us -> 0 us
  Pallas kernels: 0 us -> 31.7 us
  local copies, waits for them, and re-layouts: 19.4 us -> 2.69 us
  between operations: 14.7 us -> 1.45 us
  other arithmetic: 16 us -> 3.68 us
    all_gather x2 -> x0, blocking collectives: 164 us -> none  [the longest x1 124 us: on_device(): lax.all_gather(turned_keys, 'ctx', axis=0, tiled=True)]
    all_gather x2 -> x0, waiting for transfers between devices: 164 us -> none  [the longest x1 84.4 us: on_device(): shard_piece = lax.all_gather(turned_queries, 'ctx', axis=0, tiled=True)]
    ppermute x0 -> x20, starting transfers between devices: none -> 43.3 us  [send(): return lax.ppermute(value, 'ctx', where_to)]
    dot_general x11 -> x0, matrix products: 32.9 us -> none  [the longest x5 17.2 us: attend(): jnp.dot(weights_bf, value_slab, preferred_element_type=jnp.float32)]
    reduce_scatter x1 -> x0, waiting for transfers between devices: 32.3 us -> none  [on_device(): lax.psum_scatter(head_terms.astype(jnp.bfloat16), 'kvh', scatter_dimensio...]
    pallas_call x0 -> x5, Pallas kernels: none -> 31.7 us  [the longest x1 15.4 us: flash_second(): pl.pallas_call(functools.partial(second_kernel, chunks // 2, cache_rows),...]
    ppermute x0 -> x20, waiting for transfers between devices: none -> 21.2 us  [send(): return lax.ppermute(value, 'ctx', where_to)]
    all_to_all x1 -> x2, blocking collectives: 12.8 us -> 31.8 us  [the longest x1 19.4 us: on_device(): lax.all_to_all(partial, 'ctx', 0, 0, axis_index_groups=z_groups, tiled=True)]
  transfers between devices with their start and end apart: 5 -> 20, of which waited for: 4 -> 9; matrix products, arithmetic and copies ran while one was open for 1% -> 1% of each run, Pallas kernels for 0% -> 22%
where the time goes in v1:
time: 136 us
  starting transfers between devices  43.3 us (32%)
  blocking collectives  31.8 us (23%)
  Pallas kernels  31.7 us (23%)
  waiting for transfers between devices  21.2 us (16%)
  other arithmetic  3.68 us (3%)
  local copies, waits for them, and re-layouts  2.69 us (2%)
  between operations  1.45 us (1%)
    ppermute x20, starting transfers between devices, send(): return lax.ppermute(value, 'ctx', where_to)  43.3 us
    ppermute x20, waiting for transfers between devices, send(): return lax.ppermute(value, 'ctx', where_to)  21.2 us
    all_to_all x1, blocking collectives, on_device(): lax.all_to_all(partial, 'ctx', 0, 0, axis_index_groups=z_groups, tiled=True)  19.4 us
    pallas_call x1, Pallas kernels, flash_second(): pl.pallas_call(functools.partial(second_kernel, chunks // 2, cache_rows),...  15.4 us
    pallas_call x2, Pallas kernels, flash_first(): pl.pallas_call(functools.partial(first_kernel, chunks, cache_rows), out_s...  13.8 us
    all_to_all x1, blocking collectives, on_device(): lax.all_to_all(terms, 'kvh', 0, 0, tiled=True).astype(jnp.float32)  12.5 us
  transfers between devices with their start and end apart: 20, of which 9 were waited for; matrix products, arithmetic and copies ran while one was open for 1% of the time, Pallas kernels for 22%

profile of v1, /device:TPU:1, one launch (start us, length us, event | category | flops | bytes accessed | tf_op | source)
XLA Modules:
  0.0 135.8 jit_solution(1780100470657962308)
XLA Ops:
  1.3 1.0 bitcast_dynamic-update-slice_fusion.1
  2.3 1.0 bitcast_dynamic-update-slice_fusion
  3.3 0.9 fusion.13
  4.2 0.1 constant_dynamic-update-slice_fusion.2
  4.3 0.7 constant_dynamic-update-slice_fusion.1
  5.0 3.6 %collective-permute-start.8 = (bf16[2096,128]{1,0:T(8,128)(2,1)S(1)}, bf16[2096,128]{1,0:T(8,128)(2,1)S(1)}, u32[]{:S(2)}, u32[]{:S(2)}) collective-permute-start(bf16[2096,128]{1,0:T(8,128)(2,1)S(1)} %constant_dynamic-update-slice_fusion.refs_4_.refs_12_), channel_id=1, source_target_pairs={{0,16},{8,24},{16,0},{24,8},{32,48},{40,56},{48,32},{56,40},{64,80... | collective-permute-start | bytes 1609736 | tf_op jit(solution)/shard_map/ppermute | solution.py:300
  8.5 1.0 collective-permute-start.7
  9.5 0.1 multiply_cosine_fusion.1
  9.6 1.0 fusion.1
  10.6 0.1 maximum_bitcast_fusion
  10.8 1.7 %collective-permute-start.1 = (bf16[256,128]{1,0:T(8,128)(2,1)S(1)}, bf16[256,128]{1,0:T(8,128)(2,1)S(1)}, u32[]{:S(2)}, u32[]{:S(2)}) collective-permute-start(bf16[256,128]{1,0:T(8,128)(2,1)S(1)} %bitcast.22), channel_id=1, source_target_pairs={{0,32},{8,40},{16,48},{24,56},{32,64},{40,72},{48,80},{56,88},{64,... | collective-permute-start | bytes 196616 | tf_op jit(solution)/shard_map/ppermute | solution.py:300
  12.5 4.0 %collective-permute-start = (bf16[256,128]{1,0:T(8,128)(2,1)S(1)}, bf16[256,128]{1,0:T(8,128)(2,1)S(1)}, u32[]{:S(2)}, u32[]{:S(2)}) collective-permute-start(bf16[256,128]{1,0:T(8,128)(2,1)S(1)} %bitcast.23), channel_id=1, source_target_pairs={{0,224},{8,232},{16,240},{24,248},{32,0},{40,8},{48,16},{56,24},{6... | collective-permute-start | bytes 196616 | tf_op jit(solution)/shard_map/ppermute | solution.py:300
  16.5 0.3 collective-permute-start.18
  16.8 2.1 %collective-permute-done.1.refs_2_ = bf16[256,128]{1,0:T(8,128)(2,1)S(1)} collective-permute-done((bf16[256,128]{1,0:T(8,128)(2,1)S(1)}, bf16[256,128]{1,0:T(8,128)(2,1)S(1)}, u32[]{:S(2)}, u32[]{:S(2)}) %collective-permute-start.1) | collective-permute-done | bytes 65568 | tf_op jit(solution)/shard_map/ppermute | solution.py:300
  18.9 0.0 collective-permute-start.3
  18.9 0.5 collective-permute-done.8.refs_14_
  19.4 2.3 %collective-permute-start.9 = (bf16[2096,128]{1,0:T(8,128)(2,1)S(1)}, bf16[2096,128]{1,0:T(8,128)(2,1)}, u32[]{:S(2)}, u32[]{:S(2)}) collective-permute-start(bf16[2096,128]{1,0:T(8,128)(2,1)S(1)} %collective-permute-done.8.refs_14_), channel_id=1, source_target_pairs={{0,8},{8,0},{16,24},{24,16},{32,40},{40,32},{48,56},{56,48},{64,72... | collective-permute-start | bytes 1609736 | tf_op jit(solution)/shard_map/ppermute | solution.py:300
  21.7 0.7 and_select_fusion
  22.3 0.0 collective-permute-done.refs_1_
  22.4 5.9 %collective-permute-start.2 = (bf16[256,128]{1,0:T(8,128)(2,1)S(1)}, bf16[256,128]{1,0:T(8,128)(2,1)S(1)}, u32[]{:S(2)}, u32[]{:S(2)}) collective-permute-start(bf16[256,128]{1,0:T(8,128)(2,1)S(1)} %collective-permute-done.refs_1_), channel_id=1, source_target_pairs={{0,224},{8,232},{16,240},{24,248},{32,0},{40,8},{48,16},{56,24},{6... | collective-permute-start | bytes 196616 | tf_op jit(solution)/shard_map/ppermute | solution.py:300
  28.2 0.0 collective-permute-done.3.refs_0_.refs_4_
  28.2 0.0 collective-permute-start.5
  28.2 0.1 pad_add_fusion.where_ref
  28.3 1.4 %collective-permute-done.2.refs_3_ = bf16[256,128]{1,0:T(8,128)(2,1)S(1)} collective-permute-done((bf16[256,128]{1,0:T(8,128)(2,1)S(1)}, bf16[256,128]{1,0:T(8,128)(2,1)S(1)}, u32[]{:S(2)}, u32[]{:S(2)}) %collective-permute-start.2) | collective-permute-done | bytes 65568 | tf_op jit(solution)/shard_map/ppermute | solution.py:300
  29.8 3.4 %collective-permute-start.4 = (bf16[256,128]{1,0:T(8,128)(2,1)S(1)}, bf16[256,128]{1,0:T(8,128)(2,1)S(1)}, u32[]{:S(2)}, u32[]{:S(2)}) collective-permute-start(bf16[256,128]{1,0:T(8,128)(2,1)S(1)} %collective-permute-done.2.refs_3_), channel_id=1, source_target_pairs={{0,224},{8,232},{16,240},{24,248},{32,0},{40,8},{48,16},{56,24},{6... | collective-permute-start | bytes 196616 | tf_op jit(solution)/shard_map/ppermute | solution.py:300
  33.2 0.0 collective-permute-done.5.refs_2_.refs_6_
  33.2 0.0 collective-permute-start.6
  33.2 0.0 collective-permute-done.7.refs_5_.refs_13_
  33.2 6.9 %flash_first.2 = (f32[4,256,256]{2,1,0:T(8,128)S(1)}, f32[4,256,128]{2,1,0:T(8,128)S(1)}) custom-call(bf16[256,128]{1,0:T(8,128)(2,1)S(1)} %bitcast.24, bf16[256,128]{1,0:T(8,128)(2,1)S(1)} %collective-permute-done.refs_1_, bf16[256,128]{1,0:T(8,128)(2,1)S(1)} %collective-permute-done.1.refs_2_, bf16[256,128]{1,0:T(8,128)(2,1)S(1)} %collective-permute-done.2.refs_3_, ...), custom_call_target="tpu_custom_call" | custom-call | flops 2147483648 | bytes 4194304 | tf_op jit(solution)/shard_map/flash_first/pallas_call | solution.py:81
  40.1 0.0 collective-permute-done.4.refs_1_.refs_5_
  40.1 0.0 collective-permute-done.6.refs_3_.refs_7_
  40.1 6.9 %flash_first.3 = (f32[4,256,256]{2,1,0:T(8,128)S(1)}, f32[4,256,128]{2,1,0:T(8,128)S(1)}) custom-call(bf16[256,128]{1,0:T(8,128)(2,1)S(1)} %collective-permute-done.3.refs_0_.refs_4_, bf16[256,128]{1,0:T(8,128)(2,1)S(1)} %collective-permute-done.4.refs_1_.refs_5_, bf16[256,128]{1,0:T(8,128)(2,1)S(1)} %collective-permute-done.5.refs_2_.refs_6_, ...), custom_call_target="tpu_custom_call" | custom-call | flops 2147483648 | bytes 4194304 | tf_op jit(solution)/shard_map/flash_first/pallas_call | solution.py:81
  47.0 0.0 collective-permute-done.9.refs_15_
  47.0 0.0 copy-start
  47.1 15.4 %flash_second.1 = bf16[8,272,128]{2,1,0:T(8,128)(2,1)S(1)} custom-call(s32[11]{0:T(128)S(1)} %pad_add_fusion.where_ref, bf16[256,128]{1,0:T(8,128)(2,1)S(1)} %bitcast.25, bf16[256,128]{1,0:T(8,128)(2,1)S(1)} %collective-permute-done.refs_1_, bf16[256,128]{1,0:T(8,128)(2,1)S(1)} %collective-permute-done.1.refs_2_, ...), custom_call_target="tpu_custom_call" | custom-call | flops 4563402752 | bytes 8388608 | tf_op jit(solution)/shard_map/flash_second/pallas_call | solution.py:179
  62.5 19.4 %all_to_all.10.in_ref = bf16[8,272,128]{2,1,0:T(8,128)(2,1)S(1)} all-to-all(bf16[8,272,128]{2,1,0:T(8,128)(2,1)S(1)} %flash_second.1), channel_id=1, replica_groups={{0,32,64,96,128,160,192,224},{8,40,72,104,136,168,200,232},{16,48,80,11..., dimensions={0} | all-to-all | bytes 1114112 | tf_op jit(solution)/shard_map/all_to_all | solution.py:352
  81.8 0.5 merge.1
  82.3 2.8 %collective-permute-start.10 = (bf16[256,128]{1,0:T(8,128)(2,1)S(1)}, bf16[256,128]{1,0:T(8,128)(2,1)S(1)}, u32[]{:S(2)}, u32[]{:S(2)}) collective-permute-start(bf16[256,128]{1,0:T(8,128)(2,1)S(1)} %merge.1), channel_id=1, source_target_pairs={{0,16},{8,24},{16,0},{24,8},{32,48},{40,56},{48,32},{56,40},{64,80... | collective-permute-start | bytes 196616 | tf_op jit(solution)/shard_map/ppermute | solution.py:300
  85.1 1.9 %collective-permute-done.10 = bf16[256,128]{1,0:T(8,128)(2,1)S(1)} collective-permute-done((bf16[256,128]{1,0:T(8,128)(2,1)S(1)}, bf16[256,128]{1,0:T(8,128)(2,1)S(1)}, u32[]{:S(2)}, u32[]{:S(2)}) %collective-permute-start.10) | collective-permute-done | bytes 65568 | tf_op jit(solution)/shard_map/ppermute | solution.py:300
  87.0 0.3 collective-permute-start.12
  87.3 2.5 %collective-permute-start.11 = (bf16[512,128]{1,0:T(8,128)(2,1)S(1)}, bf16[512,128]{1,0:T(8,128)(2,1)S(1)}, u32[]{:S(2)}, u32[]{:S(2)}) collective-permute-start(bf16[512,128]{1,0:T(8,128)(2,1)S(1)} %pad_maximum_fusion.refs_0_), channel_id=1, source_target_pairs={{0,224},{8,232},{16,240},{24,248},{32,0},{40,8},{48,16},{56,24},{6... | collective-permute-start | bytes 393224 | tf_op jit(solution)/shard_map/ppermute | solution.py:300
  89.8 2.4 %collective-permute-done.12.refs_2_ = bf16[512,128]{1,0:T(8,128)(2,1)S(1)} collective-permute-done((bf16[512,128]{1,0:T(8,128)(2,1)S(1)}, bf16[512,128]{1,0:T(8,128)(2,1)S(1)}, u32[]{:S(2)}, u32[]{:S(2)}) %collective-permute-start.12) | collective-permute-done | bytes 131104 | tf_op jit(solution)/shard_map/ppermute | solution.py:300
  92.2 0.0 collective-permute-start.14
  92.2 0.0 collective-permute-done.11.refs_1_
  92.2 2.7 %collective-permute-start.13 = (bf16[512,128]{1,0:T(8,128)(2,1)S(1)}, bf16[512,128]{1,0:T(8,128)(2,1)S(1)}, u32[]{:S(2)}, u32[]{:S(2)}) collective-permute-start(bf16[512,128]{1,0:T(8,128)(2,1)S(1)} %collective-permute-done.11.refs_1_), channel_id=1, source_target_pairs={{0,224},{8,232},{16,240},{24,248},{32,0},{40,8},{48,16},{56,24},{6... | collective-permute-start | bytes 393224 | tf_op jit(solution)/shard_map/ppermute | solution.py:300
  94.8 3.9 %collective-permute-done.14.refs_4_ = bf16[512,128]{1,0:T(8,128)(2,1)S(1)} collective-permute-done((bf16[512,128]{1,0:T(8,128)(2,1)S(1)}, bf16[512,128]{1,0:T(8,128)(2,1)S(1)}, u32[]{:S(2)}, u32[]{:S(2)}) %collective-permute-start.14) | collective-permute-done | bytes 131104 | tf_op jit(solution)/shard_map/ppermute | solution.py:300
  98.8 0.0 collective-permute-start.16
  98.8 0.0 collective-permute-done.13.refs_3_
  98.8 2.7 %collective-permute-start.15 = (bf16[512,128]{1,0:T(8,128)(2,1)S(1)}, bf16[512,128]{1,0:T(8,128)(2,1)S(1)}, u32[]{:S(2)}, u32[]{:S(2)}) collective-permute-start(bf16[512,128]{1,0:T(8,128)(2,1)S(1)} %collective-permute-done.13.refs_3_), channel_id=1, source_target_pairs={{0,224},{8,232},{16,240},{24,248},{32,0},{40,8},{48,16},{56,24},{6... | collective-permute-start | bytes 393224 | tf_op jit(solution)/shard_map/ppermute | solution.py:300
  101.4 3.1 %collective-permute-done.16.refs_6_ = bf16[512,128]{1,0:T(8,128)(2,1)S(1)} collective-permute-done((bf16[512,128]{1,0:T(8,128)(2,1)S(1)}, bf16[512,128]{1,0:T(8,128)(2,1)S(1)}, u32[]{:S(2)}, u32[]{:S(2)}) %collective-permute-start.16) | collective-permute-done | bytes 131104 | tf_op jit(solution)/shard_map/ppermute | solution.py:300
  104.5 0.0 collective-permute-start.17
  104.5 0.0 collective-permute-done.18.refs_9_
  104.5 0.0 collective-permute-done.15.refs_5_
  104.5 5.0 %collective-permute-done.17.refs_7_ = bf16[512,128]{1,0:T(8,128)(2,1)S(1)} collective-permute-done((bf16[512,128]{1,0:T(8,128)(2,1)S(1)}, bf16[512,128]{1,0:T(8,128)(2,1)S(1)}, u32[]{:S(2)}, u32[]{:S(2)}) %collective-permute-start.17) | collective-permute-done | bytes 131104 | tf_op jit(solution)/shard_map/ppermute | solution.py:300
  109.6 0.0 copy-done
  109.6 2.0 %project.1 = bf16[8,32,1024]{2,1,0:T(8,128)(2,1)S(1)} custom-call(s32[11]{0:T(128)S(1)} %pad_add_fusion.where_ref, bf16[512,128]{1,0:T(8,128)(2,1)S(1)} %pad_maximum_fusion.refs_0_, bf16[512,128]{1,0:T(8,128)(2,1)S(1)} %collective-permute-done.11.refs_1_, bf16[512,128]{1,0:T(8,128)(2,1)S(1)} %collective-permute-done.12.refs_2_, ...), custom_call_target="tpu_custom_call" | custom-call | flops 1073741824 | bytes 6291456 | tf_op jit(solution)/shard_map/project/pallas_call | solution.py:258
  111.5 12.5 %all_to_all.11 = bf16[8,32,1024]{2,1,0:T(8,128)(2,1)S(1)} all-to-all(bf16[8,32,1024]{2,1,0:T(8,128)(2,1)S(1)} %project.1), channel_id=1, replica_groups=mesh['ctx'=32,'kvh'=8] {'kvh'}, dimensions={0} | all-to-all | bytes 1048576 | tf_op jit(solution)/shard_map/all_to_all | solution.py:358
  124.0 0.1 reduce_sum.12
  124.1 10.2 %collective-permute-start.19 = (bf16[32,512]{1,0:T(8,128)(2,1)S(1)}, bf16[32,512]{1,0:T(8,128)(2,1)S(1)}, u32[]{:S(2)}, u32[]{:S(2)}) collective-permute-start(bf16[32,512]{1,0:T(8,128)(2,1)S(1)} %get-tuple-element.16), channel_id=1, source_target_pairs={{0,8},{8,0},{16,24},{24,16},{32,40},{40,32},{48,56},{56,48},{64,72... | collective-permute-start | bytes 98312 | tf_op jit(solution)/shard_map/ppermute | solution.py:300
  134.3 0.9 collective-permute-done.19
  135.2 0.6 maximum_select_fusion
  (6 shorter events, 0.1 us)
Async XLA Ops:
  5.0 14.4 %collective-permute-start.8 = (bf16[2096,128]{1,0:T(8,128)(2,1)S(1)}, bf16[2096,128]{1,0:T(8,128)(2,1)S(1)}, u32[]{:S(2)}, u32[]{:S(2)}) collective-permute-start(bf16[2096,128]{1,0:T(8,128)(2,1)S(1)} %constant_dynamic-update-slice_fusion.refs_4_.refs_12_), channel_id=1, source_target_pairs={{0,16},{8,24},{16,0},{24,8},{32,48},{40,56},{48,32},{56,40},{64,80... | collective-permute-start | bytes 1609736 | tf_op jit(solution)/shard_map/ppermute | solution.py:300
  8.5 24.6 %collective-permute-start.7 = (bf16[2096,128]{1,0:T(8,128)(2,1)S(1)}, bf16[2096,128]{1,0:T(8,128)(2,1)}, u32[]{:S(2)}, u32[]{:S(2)}) collective-permute-start(bf16[2096,128]{1,0:T(8,128)(2,1)S(1)} %constant_dynamic-update-slice_fusion.refs_4_.refs_12_), channel_id=1, source_target_pairs={{0,8},{8,0},{16,24},{24,16},{32,40},{40,32},{48,56},{56,48},{64,72... | collective-permute-start | bytes 1609736 | tf_op jit(solution)/shard_map/ppermute | solution.py:300
  10.8 8.1 %collective-permute-start.1 = (bf16[256,128]{1,0:T(8,128)(2,1)S(1)}, bf16[256,128]{1,0:T(8,128)(2,1)S(1)}, u32[]{:S(2)}, u32[]{:S(2)}) collective-permute-start(bf16[256,128]{1,0:T(8,128)(2,1)S(1)} %bitcast.22), channel_id=1, source_target_pairs={{0,32},{8,40},{16,48},{24,56},{32,64},{40,72},{48,80},{56,88},{64,... | collective-permute-start | bytes 196616 | tf_op jit(solution)/shard_map/ppermute | solution.py:300
  12.5 9.9 %collective-permute-start = (bf16[256,128]{1,0:T(8,128)(2,1)S(1)}, bf16[256,128]{1,0:T(8,128)(2,1)S(1)}, u32[]{:S(2)}, u32[]{:S(2)}) collective-permute-start(bf16[256,128]{1,0:T(8,128)(2,1)S(1)} %bitcast.23), channel_id=1, source_target_pairs={{0,224},{8,232},{16,240},{24,248},{32,0},{40,8},{48,16},{56,24},{6... | collective-permute-start | bytes 196616 | tf_op jit(solution)/shard_map/ppermute | solution.py:300
  16.5 88.0 %collective-permute-start.18 = (bf16[2048,512]{1,0:T(8,128)(2,1)}, bf16[2048,512]{1,0:T(8,128)(2,1)S(1)}, u32[]{:S(2)}, u32[]{:S(2)}) collective-permute-start(bf16[2048,512]{1,0:T(8,128)(2,1)} %refs_8_.1), channel_id=1, source_target_pairs={{0,8},{8,0},{16,24},{24,16},{32,40},{40,32},{48,56},{56,48},{64,72... | collective-permute-start | bytes 6291464 | tf_op jit(solution)/shard_map/ppermute | solution.py:300
  18.9 9.3 %collective-permute-start.3 = (bf16[256,128]{1,0:T(8,128)(2,1)S(1)}, bf16[256,128]{1,0:T(8,128)(2,1)S(1)}, u32[]{:S(2)}, u32[]{:S(2)}) collective-permute-start(bf16[256,128]{1,0:T(8,128)(2,1)S(1)} %collective-permute-done.1.refs_2_), channel_id=1, source_target_pairs={{0,32},{8,40},{16,48},{24,56},{32,64},{40,72},{48,80},{56,88},{64,... | collective-permute-start | bytes 196616 | tf_op jit(solution)/shard_map/ppermute | solution.py:300
  19.4 27.6 %collective-permute-start.9 = (bf16[2096,128]{1,0:T(8,128)(2,1)S(1)}, bf16[2096,128]{1,0:T(8,128)(2,1)}, u32[]{:S(2)}, u32[]{:S(2)}) collective-permute-start(bf16[2096,128]{1,0:T(8,128)(2,1)S(1)} %collective-permute-done.8.refs_14_), channel_id=1, source_target_pairs={{0,8},{8,0},{16,24},{24,16},{32,40},{40,32},{48,56},{56,48},{64,72... | collective-permute-start | bytes 1609736 | tf_op jit(solution)/shard_map/ppermute | solution.py:300
  22.4 7.4 %collective-permute-start.2 = (bf16[256,128]{1,0:T(8,128)(2,1)S(1)}, bf16[256,128]{1,0:T(8,128)(2,1)S(1)}, u32[]{:S(2)}, u32[]{:S(2)}) collective-permute-start(bf16[256,128]{1,0:T(8,128)(2,1)S(1)} %collective-permute-done.refs_1_), channel_id=1, source_target_pairs={{0,224},{8,232},{16,240},{24,248},{32,0},{40,8},{48,16},{56,24},{6... | collective-permute-start | bytes 196616 | tf_op jit(solution)/shard_map/ppermute | solution.py:300
  28.2 4.9 %collective-permute-start.5 = (bf16[256,128]{1,0:T(8,128)(2,1)S(1)}, bf16[256,128]{1,0:T(8,128)(2,1)S(1)}, u32[]{:S(2)}, u32[]{:S(2)}) collective-permute-start(bf16[256,128]{1,0:T(8,128)(2,1)S(1)} %collective-permute-done.3.refs_0_.refs_4_), channel_id=1, source_target_pairs={{0,32},{8,40},{16,48},{24,56},{32,64},{40,72},{48,80},{56,88},{64,... | collective-permute-start | bytes 196616 | tf_op jit(solution)/shard_map/ppermute | solution.py:300
  29.8 10.3 %collective-permute-start.4 = (bf16[256,128]{1,0:T(8,128)(2,1)S(1)}, bf16[256,128]{1,0:T(8,128)(2,1)S(1)}, u32[]{:S(2)}, u32[]{:S(2)}) collective-permute-start(bf16[256,128]{1,0:T(8,128)(2,1)S(1)} %collective-permute-done.2.refs_3_), channel_id=1, source_target_pairs={{0,224},{8,232},{16,240},{24,248},{32,0},{40,8},{48,16},{56,24},{6... | collective-permute-start | bytes 196616 | tf_op jit(solution)/shard_map/ppermute | solution.py:300
  33.2 6.9 %collective-permute-start.6 = (bf16[256,128]{1,0:T(8,128)(2,1)S(1)}, bf16[256,128]{1,0:T(8,128)(2,1)S(1)}, u32[]{:S(2)}, u32[]{:S(2)}) collective-permute-start(bf16[256,128]{1,0:T(8,128)(2,1)S(1)} %collective-permute-done.5.refs_2_.refs_6_), channel_id=1, source_target_pairs={{0,32},{8,40},{16,48},{24,56},{32,64},{40,72},{48,80},{56,88},{64,... | collective-permute-start | bytes 196616 | tf_op jit(solution)/shard_map/ppermute | solution.py:300
  47.0 62.5 %copy-start = (bf16[2048,512]{1,0:T(8,128)(2,1)S(1)}, bf16[2048,512]{1,0:T(8,128)(2,1)}, u32[]{:S(2)}) copy-start(bf16[2048,512]{1,0:T(8,128)(2,1)} %refs_8_.1) | copy-start | bytes 6291460
  82.3 4.7 %collective-permute-start.10 = (bf16[256,128]{1,0:T(8,128)(2,1)S(1)}, bf16[256,128]{1,0:T(8,128)(2,1)S(1)}, u32[]{:S(2)}, u32[]{:S(2)}) collective-permute-start(bf16[256,128]{1,0:T(8,128)(2,1)S(1)} %merge.1), channel_id=1, source_target_pairs={{0,16},{8,24},{16,0},{24,8},{32,48},{40,56},{48,32},{56,40},{64,80... | collective-permute-start | bytes 196616 | tf_op jit(solution)/shard_map/ppermute | solution.py:300
  87.0 5.1 %collective-permute-start.12 = (bf16[512,128]{1,0:T(8,128)(2,1)S(1)}, bf16[512,128]{1,0:T(8,128)(2,1)S(1)}, u32[]{:S(2)}, u32[]{:S(2)}) collective-permute-start(bf16[512,128]{1,0:T(8,128)(2,1)S(1)} %pad_maximum_fusion.refs_0_), channel_id=1, source_target_pairs={{0,32},{8,40},{16,48},{24,56},{32,64},{40,72},{48,80},{56,88},{64,... | collective-permute-start | bytes 393224 | tf_op jit(solution)/shard_map/ppermute | solution.py:300
  87.3 4.8 %collective-permute-start.11 = (bf16[512,128]{1,0:T(8,128)(2,1)S(1)}, bf16[512,128]{1,0:T(8,128)(2,1)S(1)}, u32[]{:S(2)}, u32[]{:S(2)}) collective-permute-start(bf16[512,128]{1,0:T(8,128)(2,1)S(1)} %pad_maximum_fusion.refs_0_), channel_id=1, source_target_pairs={{0,224},{8,232},{16,240},{24,248},{32,0},{40,8},{48,16},{56,24},{6... | collective-permute-start | bytes 393224 | tf_op jit(solution)/shard_map/ppermute | solution.py:300
  92.2 6.6 %collective-permute-start.14 = (bf16[512,128]{1,0:T(8,128)(2,1)S(1)}, bf16[512,128]{1,0:T(8,128)(2,1)S(1)}, u32[]{:S(2)}, u32[]{:S(2)}) collective-permute-start(bf16[512,128]{1,0:T(8,128)(2,1)S(1)} %collective-permute-done.12.refs_2_), channel_id=1, source_target_pairs={{0,32},{8,40},{16,48},{24,56},{32,64},{40,72},{48,80},{56,88},{64,... | collective-permute-start | bytes 393224 | tf_op jit(solution)/shard_map/ppermute | solution.py:300
  92.2 6.6 %collective-permute-start.13 = (bf16[512,128]{1,0:T(8,128)(2,1)S(1)}, bf16[512,128]{1,0:T(8,128)(2,1)S(1)}, u32[]{:S(2)}, u32[]{:S(2)}) collective-permute-start(bf16[512,128]{1,0:T(8,128)(2,1)S(1)} %collective-permute-done.11.refs_1_), channel_id=1, source_target_pairs={{0,224},{8,232},{16,240},{24,248},{32,0},{40,8},{48,16},{56,24},{6... | collective-permute-start | bytes 393224 | tf_op jit(solution)/shard_map/ppermute | solution.py:300
  98.8 5.8 %collective-permute-start.16 = (bf16[512,128]{1,0:T(8,128)(2,1)S(1)}, bf16[512,128]{1,0:T(8,128)(2,1)S(1)}, u32[]{:S(2)}, u32[]{:S(2)}) collective-permute-start(bf16[512,128]{1,0:T(8,128)(2,1)S(1)} %collective-permute-done.14.refs_4_), channel_id=1, source_target_pairs={{0,32},{8,40},{16,48},{24,56},{32,64},{40,72},{48,80},{56,88},{64,... | collective-permute-start | bytes 393224 | tf_op jit(solution)/shard_map/ppermute | solution.py:300
  98.8 5.8 %collective-permute-start.15 = (bf16[512,128]{1,0:T(8,128)(2,1)S(1)}, bf16[512,128]{1,0:T(8,128)(2,1)S(1)}, u32[]{:S(2)}, u32[]{:S(2)}) collective-permute-start(bf16[512,128]{1,0:T(8,128)(2,1)S(1)} %collective-permute-done.13.refs_3_), channel_id=1, source_target_pairs={{0,224},{8,232},{16,240},{24,248},{32,0},{40,8},{48,16},{56,24},{6... | collective-permute-start | bytes 393224 | tf_op jit(solution)/shard_map/ppermute | solution.py:300
  104.5 5.0 %collective-permute-start.17 = (bf16[512,128]{1,0:T(8,128)(2,1)S(1)}, bf16[512,128]{1,0:T(8,128)(2,1)S(1)}, u32[]{:S(2)}, u32[]{:S(2)}) collective-permute-start(bf16[512,128]{1,0:T(8,128)(2,1)S(1)} %collective-permute-done.16.refs_6_), channel_id=1, source_target_pairs={{0,32},{8,40},{16,48},{24,56},{32,64},{40,72},{48,80},{56,88},{64,... | collective-permute-start | bytes 393224 | tf_op jit(solution)/shard_map/ppermute | solution.py:300
  124.1 11.1 %collective-permute-start.19 = (bf16[32,512]{1,0:T(8,128)(2,1)S(1)}, bf16[32,512]{1,0:T(8,128)(2,1)S(1)}, u32[]{:S(2)}, u32[]{:S(2)}) collective-permute-start(bf16[32,512]{1,0:T(8,128)(2,1)S(1)} %get-tuple-element.16), channel_id=1, source_target_pairs={{0,8},{8,0},{16,24},{24,16},{32,40},{40,32},{48,56},{56,48},{64,72... | collective-permute-start | bytes 98312 | tf_op jit(solution)/shard_map/ppermute | solution.py:300
